TPU v7x, 32 devices: a whole 2x2x4 slice. The times are simulated.
32 devices in a mesh: seq: 4 (over y, x), frame: 8 (over z, core).
Axes of the slice: x: 2, y: 2, z: 4, core: 2. Of those that a mesh axis runs over, the one named last changes fastest.
Arguments:
- value_grad: bfloat16 [8, 4096, 512], P('frame', 'seq'), may hold values from -6 to 6
- w_value: bfloat16 [8192, 512], P('seq'), may hold values from -0.25 to 0.25
- norm_gain: float32 [8192], P('seq'), may hold values from 0.1 to 1.9
- vis_pos: int32 [8, 128], P('frame'), may hold values from 0 to 4095, as said below
- frame_owner: int32 [8, 128, 1], P('frame'), may hold values from 0 to 7; in each aligned block of 128 rows (0 to 127, 128 to 255, ..., all dimensions but the last counted through in order) at most 32 rows name the same one
- ques_span: int32 [8, 2], P('frame'), may hold values from 0 to 32, as said below
- vis_proj: bfloat16 [8, 128, 8192], P('frame', None, 'seq')
- vis_resid: bfloat16 [8, 128, 8192], P('frame', None, 'seq'), may hold values from -6 to 6
- ques_hidden: bfloat16 [8, 32, 8192], P('frame', None, 'seq'), may hold values from -6 to 6
- w_down: bfloat16 [8192, 8192], P(None, 'seq'), may hold values from -0.0625 to 0.0625
- pre_owned: bfloat16 [8, 8192, 256], P('frame', 'seq'), may hold values from -6 to 6
Outputs:
- pre_grad: bfloat16 [8, 8192, 256], P('frame', 'seq')
- ques_grad: bfloat16 [8, 32, 8192], P('frame', None, 'seq')
Inputs may be any that keep to these rules, and one draw needn't show every extreme that they name: `vis_pos`: each row is distinct and increasing. `frame_owner`: in each sequence at most 32 visual tokens name the same owner. `ques_span`: column 1 is at least 1, and column 0 plus column 1 is at most 32.
All inputs are finite; a program needn't handle non-finite values.
Results may differ from a plain program's by a relative error of at most 0.015.
Values may be sent and summed in bfloat16 or wider, within the bound.
No kernel may reach another device: no remote copies, remote signals or barrier semaphores. Data moves between devices by JAX's collectives and lax.ppermute only.
A program may use at most 128 MiB of HBM per device.

v0:
```python
import math

import jax
import jax.numpy as jnp
from jax import lax
from jax.sharding import PartitionSpec as P

D = 8192


epsilon = 1e-06


def gelu_slope(pre_act):
    normal_cdf = 0.5 * (1.0 + lax.erf(pre_act * 0.7071067811865476))
    density = jnp.exp(-0.5 * pre_act * pre_act) * 0.3989422804014327
    return normal_cdf + pre_act * density


def body(
    value_grad,
    w_value,
    norm_gain,
    vis_pos,
    frame_owner,
    ques_span,
    vis_proj,
    vis_resid,
    ques_hidden,
    w_down,
    pre_owned,
):
    positions = vis_pos[0]
    local_rows = value_grad[0]
    shard_len = local_rows.shape[0]
    projected = vis_proj[0].astype(jnp.float32)
    residual = vis_resid[0].astype(jnp.float32)
    span_start = ques_span[0, 0]
    span_count = ques_span[0, 1]
    places = jnp.arange(ques_hidden.shape[1], dtype=jnp.int32)
    span_mask = ((places >= span_start) & (places < span_start + span_count)).astype(jnp.float32)
    count_value = span_count.astype(jnp.float32)
    quest_mean = (
        jnp.dot(
            span_mask.astype(jnp.bfloat16)[None, :],
            ques_hidden[0],
            preferred_element_type=jnp.float32,
        )[0]
        / count_value
    )
    sum_query = jnp.sum(projected * quest_mean[None, :], axis=1)
    sum_square = jnp.sum(projected * projected, axis=1)
    sum_query, sum_square = lax.psum((sum_query, sum_square), "seq")
    offset = lax.axis_index("seq") * shard_len
    token_index = offset + jnp.arange(shard_len, dtype=jnp.int32)
    select = (positions[:, None] == token_index[None, :]).astype(jnp.bfloat16)
    own_rows = jnp.dot(select, local_rows, preferred_element_type=jnp.float32)
    own_piece = own_rows.astype(jnp.bfloat16)[None]
    picked = jnp.sum(
        lax.all_gather(own_piece, "seq", axis=0, tiled=True).astype(jnp.float32), axis=0
    )
    normed_grad = jnp.einsum(
        "jk,dk->jd", picked.astype(jnp.bfloat16), w_value, preferred_element_type=jnp.float32
    )
    sum_norm = jnp.sum(norm_gain[None, :] * normed_grad * projected, axis=1)
    sum_resid = jnp.sum(residual * projected, axis=1)
    sum_norm, sum_resid = lax.psum((sum_norm, sum_resid), "seq")
    gate_scale = 4.0 / math.sqrt(D)
    gate_value = jax.nn.sigmoid(gate_scale * sum_query)
    inv_rms = lax.rsqrt(gate_value * gate_value * sum_square / D + epsilon)
    inner_sum = gate_value * sum_norm
    coef_value = gate_value * inv_rms * inv_rms * inv_rms * inner_sum / D
    input_grad = (
        residual
        + inv_rms[:, None] * norm_gain[None, :] * normed_grad
        - coef_value[:, None] * projected
    )
    gate_grad = sum_resid + inv_rms * sum_norm - coef_value * sum_square
    logit_grad = gate_grad * gate_value * (1.0 - gate_value)
    proj_grad = (
        gate_value[:, None] * input_grad + (logit_grad * gate_scale)[:, None] * quest_mean[None, :]
    ).astype(jnp.bfloat16)
    quest_grad = jnp.sum((logit_grad * gate_scale)[:, None] * projected, axis=0)
    ques_out = (span_mask[:, None] * quest_grad[None, :] / count_value).astype(jnp.bfloat16)[None]
    owners_count = lax.axis_size("frame")
    slot_total = pre_owned.shape[2]
    capacity = slot_total // owners_count
    owners = frame_owner[0, :, 0]
    owner_hot = (owners[:, None] == jnp.arange(owners_count, dtype=jnp.int32)[None, :]).astype(
        jnp.int32
    )
    earlier = jnp.cumsum(owner_hot, axis=0) - owner_hot
    rank_in_owner = jnp.sum(earlier * owner_hot, axis=1)
    targets = owners * capacity + rank_in_owner
    placing = (jnp.arange(slot_total, dtype=jnp.int32)[:, None] == targets[None, :]).astype(
        jnp.bfloat16
    )
    outgoing = jnp.dot(placing, proj_grad, preferred_element_type=jnp.float32).astype(jnp.bfloat16)
    incoming = lax.all_to_all(outgoing, "frame", split_axis=0, concat_axis=0, tiled=True)
    hidden_sum = lax.psum_scatter(
        jnp.einsum("hd,nd->hn", w_down, incoming, preferred_element_type=jnp.float32).astype(
            jnp.bfloat16
        ),
        "seq",
        scatter_dimension=0,
        tiled=True,
    ).astype(jnp.float32)
    pre_act = pre_owned[0].astype(jnp.float32)
    pre_out = (hidden_sum * gelu_slope(pre_act)).astype(jnp.bfloat16)[None]
    return (pre_out, ques_out)


def solution(mesh):
    in_specs = (
        P("frame", "seq", None),
        P("seq", None),
        P("seq"),
        P("frame", None),
        P("frame", None, None),
        P("frame", None),
        P("frame", None, "seq"),
        P("frame", None, "seq"),
        P("frame", None, "seq"),
        P(None, "seq"),
        P("frame", "seq", None),
    )
    out_specs = (P("frame", "seq", None), P("frame", None, "seq"))
    return jax.shard_map(body, mesh=mesh, in_specs=in_specs, out_specs=out_specs, check_vma=False)
```

profile of v0, /device:TPU:0, one launch (start us, length us, event | category | flops | bytes accessed | tf_op | source)
XLA Modules:
  0.0 150.9 jit_solution(36403121159231280)
XLA Ops:
  7.2 0.0 copy-start
  7.2 0.0 copy-start.5
  7.2 0.0 reduce-scatter.2.cloned.1.call-start
  7.3 1.4 fusion.40
  10.6 0.6 and_convert_fusion
  11.3 1.6 %convolution_convert_fusion.2 = bf16[128,512]{1,0:T(8,128)(2,1)S(1)} fusion(bf16[1,1024,512]{2,1,0:T(8,128)(2,1)} %param.11, s32[1024]{0:T(1024)S(1)} %iota_add_fusion, s32[128]{0:T(128)} %bitcast.55), kind=kOutput, calls=%fused_computation.22 | convolution fusion | flops 134414336 | bytes 1184256 | tf_op jit(solution)/shard_map/dot_general | solution.py:57
  12.9 11.5 %all-gather = bf16[512,512]{1,0:T(8,128)(2,1)S(1)} all-gather(bf16[128,512]{1,0:T(8,128)(2,1)S(1)} %convolution_convert_fusion.2), channel_id=2, replica_groups=mesh['seq'=4,'frame'=8] {'seq'}, dimensions={0}, use_global_device_ids=true | all-gather | bytes 655360 | tf_op jit(solution)/shard_map/all_gather | solution.py:60
  24.4 0.7 fusion.35
  25.1 0.2 reduce_window_sum.11
  25.3 0.8 select_reduce_fusion
  26.2 0.1 fusion.32
  26.3 0.1 reduce_sum.69
  26.4 2.9 %fusion.15 = (f32[128]{0:T(128)S(1)}, f32[128]{0:T(128)S(1)}, f32[128]{0:T(128)S(1)}, f32[128]{0:T(128)S(1)}, f32[128,2048]{1,0:T(8,128)}) fusion(bf16[1,128,2048]{2,1,0:T(8,128)(2,1)S(1)} %copy-done.1, f32[2048]{0:T(1024)S(1)} %copy-done.4, bf16[1,128,2048]{2,1,0:T(8,128)(2,1)} %param.18, f32[2048]{0:T(1024)S(1)} %broadcast_divide_fusion, ...), kind=kOutput, calls=%fused_computation.29 | convolution fusion | flops 271318528 | bytes 4343808 | tf_op jit(solution)/shard_map/jk,dk->jd/dot_general | solution.py:62
  29.4 8.9 %all-reduce = (f32[128]{0:T(128)S(1)}, f32[128]{0:T(128)S(1)}, f32[128]{0:T(128)S(1)}, f32[128]{0:T(128)S(1)}) all-reduce(f32[128]{0:T(128)S(1)} %get-tuple-element.7, f32[128]{0:T(128)S(1)} %get-tuple-element.6, f32[128]{0:T(128)S(1)} %get-tuple-element.5, f32[128]{0:T(128)S(1)} %get-tuple-element.4), channel_id=1, replica_groups=mesh['seq'=4,'frame'=8] {'seq'}, use_global_device_ids=true, to_apply=%region_3.0 | all-reduce | flops 512 | bytes 4096 | tf_op jit(solution)/shard_map/psum | solution.py:53
  38.4 1.9 %convolution_convert_fusion.1 = bf16[256,2048]{1,0:T(8,128)(2,1)S(1)} fusion(f32[128,2048]{1,0:T(8,128)} %get-tuple-element.18, bf16[1,128,2048]{2,1,0:T(8,128)(2,1)S(1)} %copy-done.2, bf16[1,128,2048]{2,1,0:T(8,128)(2,1)S(1)} %copy-done.1, f32[128]{0:T(128)S(1)} %get-tuple-element.15, f32[128]{0:T(128)S(1)} %get-tuple-element.14, f32[2048]{0:T(1024)S(1)} %copy-done.4, ...), kind=kOutput, calls=%fused_computation.6 | convolution fusion | flops 137658368 | bytes 3164672 | tf_op jit(solution)/shard_map/dot_general | solution.py:98
  40.3 31.3 %all_to_all.12 = bf16[8,32,2048]{2,1,0:T(8,128)(2,1)S(1)} all-to-all(bf16[8,32,2048]{2,1,0:T(8,128)(2,1)S(1)} %bitcast.49), channel_id=1, replica_groups=mesh['seq'=4,'frame'=8] {'frame'}, dimensions={0} | all-to-all | bytes 2097152 | tf_op jit(solution)/shard_map/all_to_all | solution.py:99
  71.5 16.6 %fusion = bf16[8192,256]{0,1:T(8,128)(2,1)} fusion(bf16[256,2048]{1,0:T(8,128)(2,1)S(1)} %bitcast.51, bf16[8192,2048]{1,0:T(8,128)(2,1)} %param.20), kind=kOutput, calls=%fused_computation.1 | convolution fusion | flops 8592031744 | bytes 38797312 | tf_op jit(solution)/shard_map/hd,nd->hn/dot_general | solution.py:101
  88.1 0.0 reduce-scatter.2.cloned.1.call-update
  88.2 1.5 copy.13
  89.7 1.2 fusion.17
  90.9 0.8 divide_convert_fusion
  91.6 47.3 %reduce-scatter.2.cloned.1.call-done = bf16[2048,256]{0,1:T(8,128)(2,1)} async-done(((bf16[8192,256]{0,1:T(8,128)(2,1)}), bf16[2048,256]{0,1:T(8,128)(2,1)}) %reduce-scatter.2.cloned.1.call-update) | async-done | bytes 1048592 | tf_op jit(solution)/shard_map/reduce_scatter | solution.py:100
  139.0 2.9 %fusion.19 = bf16[1,2048,256]{1,2,0:T(8,128)(2,1)} fusion(bf16[1,2048,256]{1,2,0:T(8,128)(2,1)S(1)} %copy.13, bf16[2048,256]{0,1:T(8,128)(2,1)} %reduce-scatter.2.cloned.1.call-done), kind=kLoop, calls=%fused_computation.33 | loop fusion | flops 6291456 | bytes 3145728 | tf_op jit(solution)/shard_map/broadcast_in_dim | solution.py:109
  141.8 2.3 %copy.14 = bf16[1,2048,256]{2,1,0:T(8,128)(2,1)} copy(bf16[1,2048,256]{1,2,0:T(8,128)(2,1)} %fusion.19) | data formatting | bytes 2097152
  (15 shorter events, 0.1 us)
Async XLA Ops:
  7.2 19.2 %copy-start = (bf16[2048,512]{1,0:T(8,128)(2,1)S(1)}, bf16[2048,512]{1,0:T(8,128)(2,1)}, u32[]{:S(2)}) copy-start(bf16[2048,512]{1,0:T(8,128)(2,1)} %param.12) | copy-start | bytes 6291460
  7.2 19.0 %copy-start.5 = (s32[1,128,1]{1,2,0:T(1,128)S(1)}, s32[1,128,1]{1,2,0:T(1,128)}, u32[]{:S(2)}) copy-start(s32[1,128,1]{1,2,0:T(1,128)} %param.15) | copy-start | bytes 1540
  7.2 19.0 %copy-start.3 = (bf16[1,32,2048]{2,1,0:T(8,128)(2,1)S(1)}, bf16[1,32,2048]{2,1,0:T(8,128)(2,1)}, u32[]{:S(2)}) copy-start(bf16[1,32,2048]{2,1,0:T(8,128)(2,1)} %param.19) | copy-start | bytes 393220
  7.2 19.2 %copy-start.4 = (f32[2048]{0:T(1024)S(1)}, f32[2048]{0:T(1024)}, u32[]{:S(2)}) copy-start(f32[2048]{0:T(1024)} %param.13) | copy-start | bytes 24580
  7.2 19.2 %copy-start.1 = (bf16[1,128,2048]{2,1,0:T(8,128)(2,1)S(1)}, bf16[1,128,2048]{2,1,0:T(8,128)(2,1)}, u32[]{:S(2)}) copy-start(bf16[1,128,2048]{2,1,0:T(8,128)(2,1)} %param.17) | copy-start | bytes 1572868
  7.2 131.7 %reduce-scatter.2.cloned.1.call-start = ((), (), s32[]{:S(2)}) async-start(), calls=%async_computation.2 | async-start | bytes 5242880 | tf_op jit(solution)/shard_map/reduce_scatter | solution.py:100
  26.4 11.9 %copy-start.2 = (bf16[1,128,2048]{2,1,0:T(8,128)(2,1)S(1)}, bf16[1,128,2048]{2,1,0:T(8,128)(2,1)}, u32[]{:S(2)}) copy-start(bf16[1,128,2048]{2,1,0:T(8,128)(2,1)} %param.18) | copy-start | bytes 1572868
Sparse Core Ops, SparseCore 0:
  88.3 50.6 reduce-scatter.1
where the time goes:
time: 151 us
  blocking collectives  51.7 us (34%)
  waiting for transfers between devices  47.3 us (31%)
  matrix products  23.2 us (15%)
  between operations  16.2 us (11%)
  other arithmetic  7.35 us (5%)
  local copies, waits for them, and re-layouts  5.19 us (3%)
    reduce_scatter x1, waiting for transfers between devices, body(): lax.psum_scatter(jnp.einsum('hd,nd->hn', w_down, incoming, preferred_elem...  47.3 us
    all_to_all x1, blocking collectives, body(): lax.all_to_all(outgoing, 'frame', split_axis=0, concat_axis=0, tiled=True)  31.3 us
    dot_general x1, matrix products, body(): jnp.einsum('hd,nd->hn', w_down, incoming, preferred_element_type=jnp.floa...  16.6 us
    all_gather x1, blocking collectives, body(): lax.all_gather(own_piece, 'seq', axis=0, tiled=True).astype(jnp.float32)  11.5 us
    psum x1, blocking collectives, body(): sum_query, sum_square = lax.psum((sum_query, sum_square), 'seq')  8.94 us
    unnamed x14, local copies, waits for them, and re-layouts  3.78 us
  transfers between devices with their start and end apart: 1, of which 1 were waited for; matrix products, arithmetic and copies ran while one was open for 2% of the time, Pallas kernels for 0%

commit v1 on v0

v1 whole, which is shorter than its diff:
```python
import functools
import math

import jax
import jax.numpy as jnp
from jax import lax
from jax.experimental import pallas as pl
from jax.experimental.pallas import tpu as pltpu
from jax.sharding import PartitionSpec as P

EPSILON = 1e-06
F32 = jnp.float32
BF16 = jnp.bfloat16
LANES = 128
VMEM_BYTES = 40 * 1024 * 1024
HBM = pl.BlockSpec(memory_space=pltpu.HBM)
VMEM = pl.BlockSpec(memory_space=pltpu.VMEM)
ANY = pl.BlockSpec(memory_space=pl.ANY)


def call(kernel, out_shape, in_specs, scratch=(), aliases=None, out_specs=None):
    return pl.pallas_call(
        kernel,
        out_shape=out_shape,
        in_specs=in_specs,
        out_specs=jax.tree.map(lambda _: VMEM, out_shape) if out_specs is None else out_specs,
        scratch_shapes=list(scratch),
        input_output_aliases=aliases or {},
        compiler_params=pltpu.CompilerParams(vmem_limit_bytes=VMEM_BYTES),
        cost_estimate=pl.CostEstimate(flops=1024, bytes_accessed=1024, transcendentals=0),
    )


def shape(dims, dtype):
    return jax.ShapeDtypeStruct(dims, dtype)


def swap(value, axis, count, step):
    return lax.ppermute(value, axis, [(i, i ^ step) for i in range(count)])


def to_column(row):
    return jnp.transpose(jnp.broadcast_to(row, (LANES, row.shape[1])), (1, 0))


def pick_kernel(pieces, pos_hbm, rows_hbm, own_ref, pos, rows, sems):
    tokens, shard_len = pos.shape[1], rows.shape[0]
    size = shard_len // pieces
    head = pltpu.make_async_copy(pos_hbm, pos, sems.at[pieces])
    head.start()
    copies = []
    for piece in range(pieces):
        cut = pl.ds(piece * size, size)
        copies.append(
            pltpu.make_async_copy(rows_hbm.at[0, cut], rows.at[cut], sems.at[piece])
        )
        copies[-1].start()
    offset = lax.axis_index("seq") * shard_len
    head.wait()
    column = to_column(pos[...] - offset)
    lanes = lax.broadcasted_iota(jnp.int32, (tokens, LANES), 1)
    total = None
    for piece in range(pieces):
        select = jnp.concatenate(
            [
                jnp.where(column == lanes + at, 1.0, 0.0).astype(BF16)
                for at in range(piece * size, (piece + 1) * size, LANES)
            ],
            axis=1,
        )
        copies[piece].wait()
        part = jnp.dot(
            select, rows[piece * size : (piece + 1) * size, :], preferred_element_type=F32
        )
        total = part if total is None else total + part
    own_ref[...] = total.astype(BF16)


def load_kernel(
    span_hbm, hidden_hbm, gain_hbm, proj_hbm, resid_hbm, weight_hbm,
    stats_ref, projt_ref, residt_ref, gaint_ref, meant_ref, weight_ref,
    span, hidden, gain, proj, resid, sems,
):
    copies = [
        pltpu.make_async_copy(source, target, sems.at[index])
        for index, (source, target) in enumerate(
            [
                (span_hbm, span),
                (hidden_hbm.at[0], hidden),
                (gain_hbm, gain),
                (proj_hbm.at[0], proj),
                (resid_hbm.at[0], resid),
                (weight_hbm, weight_ref),
            ]
        )
    ]
    for copy in copies:
        copy.start()
    for copy in copies[:5]:
        copy.wait()
    start, count = span[0, 0], span[0, 1]
    tokens, width = proj.shape
    places = lax.broadcasted_iota(jnp.int32, (hidden.shape[0], 1), 0)
    mask = ((places >= start) & (places < start + count)).astype(F32)
    query = square = cross = jnp.zeros((LANES, tokens), F32)
    for at in range(0, width, LANES):
        cut = slice(at, at + LANES)
        mean = jnp.sum(hidden[:, cut].astype(F32) * mask, axis=0, keepdims=True)
        meant = to_column(mean / count.astype(F32))
        projt = jnp.transpose(proj[:, cut].astype(F32), (1, 0))
        residt = jnp.transpose(resid[:, cut].astype(F32), (1, 0))
        meant_ref[cut, :] = meant
        projt_ref[cut, :] = projt
        residt_ref[cut, :] = residt
        gaint_ref[cut, :] = to_column(gain[:, cut])
        query = query + projt * meant
        square = square + projt * projt
        cross = cross + projt * residt
    stats_ref[...] = jnp.zeros(stats_ref.shape, F32)
    for row, value in enumerate((query, square, cross)):
        stats_ref[row : row + 1, :] = jnp.sum(value, axis=0, keepdims=True)
    copies[5].wait()


def norm_kernel(peers, *refs):
    own_refs = refs[:peers]
    stats_ref, weight_ref, gaint_ref, projt_ref, scaledt_ref, sums_ref, pickedt = refs[peers:]
    key_width = own_refs[0].shape[1]
    for at in range(0, key_width, LANES):
        cut = slice(at, at + LANES)
        picked = own_refs[0][:, cut].astype(F32)
        for ref in own_refs[1:]:
            picked = picked + ref[:, cut].astype(F32)
        pickedt[cut, :] = jnp.transpose(picked, (1, 0)).astype(BF16)
    width, tokens = projt_ref.shape
    total = jnp.zeros((LANES, tokens), F32)
    for at in range(0, width, 256):
        cut = slice(at, at + 256)
        normed = jnp.dot(weight_ref[cut, :], pickedt[...], preferred_element_type=F32)
        scaled = normed * gaint_ref[cut, :]
        scaledt_ref[cut, :] = scaled
        terms = scaled * projt_ref[cut, :]
        total = total + terms[:LANES] + terms[LANES:]
    sums_ref[...] = stats_ref[...]
    sums_ref[3:4, :] = jnp.sum(total, axis=0, keepdims=True)


def start_weights(weight_hbm, weights, sems, peers, base, rows):
    quarter = weight_hbm.shape[0] // peers
    block = min(rows, 256)
    copies = []
    for peer in range(peers):
        first = (lax.axis_index("seq") ^ peer) * quarter + base
        for at in range(0, rows, block):
            index = len(copies)
            copies.append(
                pltpu.make_async_copy(
                    weight_hbm.at[pl.ds(pl.multiple_of(first + at, block), block)],
                    weights.at[pl.ds(peer * rows + at, block)],
                    sems.at[index],
                )
            )
            copies[-1].start()
    return copies


def multiply(weights, copies, gradt_ref, out_refs):
    rows = out_refs[0].shape[0]
    block = min(rows, 256)
    inner = rows // block
    for index, copy in enumerate(copies):
        peer, part = index // inner, index % inner
        copy.wait()
        value = jnp.dot(
            weights[index * block : (index + 1) * block, :],
            gradt_ref[...],
            preferred_element_type=F32,
        )
        out_refs[peer][part * block : (part + 1) * block, :] = value.astype(BF16)


def gate_kernel(features, peers, base, rows, *refs):
    sums_refs = refs[:peers]
    projt_ref, residt_ref, scaledt_ref, meant_ref, weight_hbm = refs[peers : peers + 5]
    gradt_ref, logit_ref = refs[peers + 5 : peers + 7]
    out_refs = refs[peers + 7 : -2]
    weights, sems = refs[-2:]
    copies = start_weights(weight_hbm, weights, sems, peers, base, rows)
    sums = sums_refs[0][...]
    for ref in sums_refs[1:]:
        sums = sums + ref[...]
    sum_query, sum_square, sum_resid, sum_norm = (sums[i : i + 1] for i in range(4))
    gate_scale = 4.0 / math.sqrt(features)
    gate = jax.nn.sigmoid(gate_scale * sum_query)
    inv_rms = lax.rsqrt(gate * gate * sum_square / features + EPSILON)
    coef = gate * inv_rms * inv_rms * inv_rms * (gate * sum_norm) / features
    gate_grad = sum_resid + inv_rms * sum_norm - coef * sum_square
    logit = gate_grad * gate * (1.0 - gate) * gate_scale
    logit_ref[...] = jnp.broadcast_to(logit, logit_ref.shape)
    for at in range(0, projt_ref.shape[0], LANES):
        cut = slice(at, at + LANES)
        grad = residt_ref[cut, :] + inv_rms * scaledt_ref[cut, :] - coef * projt_ref[cut, :]
        gradt_ref[cut, :] = (gate * grad + logit * meant_ref[cut, :]).astype(BF16)
    multiply(weights, copies, gradt_ref, out_refs)


def down_kernel(peers, base, rows, after, *refs):
    weight_hbm, gradt_ref = refs[:2]
    out_refs = refs[2 + after : -2]
    weights, sems = refs[-2:]
    copies = start_weights(weight_hbm, weights, sems, peers, base, rows)
    multiply(weights, copies, gradt_ref, out_refs)


def ques_kernel(span_hbm, logit_ref, proj_hbm, after_ref, out_ref, span, proj, sems):
    del after_ref
    head = pltpu.make_async_copy(span_hbm, span, sems.at[0])
    load = pltpu.make_async_copy(proj_hbm.at[0], proj, sems.at[1])
    head.start()
    load.start()
    head.wait()
    start, count = span[0, 0], span[0, 1]
    length, width = out_ref.shape[1], out_ref.shape[2]
    places = lax.broadcasted_iota(jnp.int32, (length, LANES), 0)
    mask = ((places >= start) & (places < start + count)).astype(F32)
    column = to_column(logit_ref[0:1, :])
    load.wait()
    for at in range(0, width, LANES):
        cut = slice(at, at + LANES)
        total = jnp.sum(column * proj[:, cut].astype(F32), axis=0, keepdims=True)
        out_ref[0, :, cut] = (mask * total / count.astype(F32)).astype(BF16)


def place_kernel(capacity, owners_count, halves, mine, *refs):
    owner_hbm = refs[0]
    part_refs = refs[1 : 1 + mine]
    out_refs = refs[-2 - halves : -2]
    owner_ref, sem = refs[-2:]
    head = pltpu.make_async_copy(owner_hbm, owner_ref, sem.at[0])
    head.start()
    head.wait()
    tokens = owner_ref.shape[1]
    owner = owner_ref[...]
    column = to_column(owner)
    above = lax.broadcasted_iota(jnp.int32, (tokens, tokens), 0)
    below = lax.broadcasted_iota(jnp.int32, (tokens, tokens), 1)
    earlier = jnp.where((column == owner) & (above < below), 1.0, 0.0)
    rank = jnp.sum(earlier, axis=0, keepdims=True).astype(jnp.int32)
    away = owner ^ lax.axis_index("frame")
    if halves == 2:
        away = (away & 1) * (owners_count // 2) + (away >> 1)
    target = away * capacity + rank
    slots = owners_count * capacity
    places = lax.broadcasted_iota(jnp.int32, (slots, tokens), 0)
    placing = jnp.where(places == target, 1.0, 0.0).astype(BF16)
    total = part_refs[0][...].astype(F32)
    for ref in part_refs[1:]:
        total = total + ref[...].astype(F32)
    placed = lax.dot_general(
        placing, total.astype(BF16), (((1,), (1,)), ((), ())), preferred_element_type=F32
    ).astype(BF16)
    size = slots // halves
    for index, ref in enumerate(out_refs):
        ref[...] = placed[index * size : (index + 1) * size, :]


def group_kernel(capacity, same_ref, other_ref, *out_refs):
    for index, ref in enumerate(out_refs):
        cut = slice(index * capacity, (index + 1) * capacity)
        ref[:capacity, :] = same_ref[cut, :]
        ref[capacity:, :] = other_ref[cut, :]


def slope(pre_act):
    normal_cdf = 0.5 * (1.0 + lax.erf(pre_act * 0.7071067811865476))
    density = jnp.exp(-0.5 * pre_act * pre_act) * 0.3989422804014327
    return normal_cdf + pre_act * density


def final_kernel(capacity, base, count, *refs):
    part_refs = refs[:count]
    pre_hbm = refs[count]
    out_hbm, pre, out, sems = refs[-4:]
    rows, slots = pre.shape
    cut = pl.ds(base, rows)
    load = pltpu.make_async_copy(pre_hbm.at[0, cut], pre, sems.at[0])
    load.start()
    joined = jnp.concatenate([ref[...] for ref in part_refs], axis=0)
    source = lax.broadcasted_iota(jnp.int32, (slots, slots), 0)
    goal = lax.broadcasted_iota(jnp.int32, (slots, slots), 1)
    moved = (goal ^ (lax.axis_index("frame") * capacity)) == source
    hidden = lax.dot_general(
        joined,
        jnp.where(moved, 1.0, 0.0).astype(BF16),
        (((0,), (0,)), ((), ())),
        preferred_element_type=F32,
    )
    load.wait()
    out[...] = (hidden * slope(pre[...].astype(F32))).astype(BF16)
    store = pltpu.make_async_copy(out, out_hbm.at[0, cut], sems.at[1])
    store.start()
    store.wait()


def chunk_rows(quarter):
    if quarter % 2048 == 0:
        return [quarter // 4, 3 * quarter // 8, 3 * quarter // 8]
    return [quarter // 2] * 2


def body(
    peers,
    owners_count,
    value_grad,
    w_value,
    norm_gain,
    vis_pos,
    frame_owner,
    ques_span,
    vis_proj,
    vis_resid,
    ques_hidden,
    w_down,
    pre_owned,
):
    _, tokens, width = vis_proj.shape
    shard_len, key_width = value_grad.shape[1:]
    length = ques_hidden.shape[1]
    features = peers * width
    slots = pre_owned.shape[2]
    capacity = slots // owners_count
    gain = norm_gain.reshape(1, width)
    owner = frame_owner.reshape(1, tokens)
    row = shape((8, tokens), F32)
    tall = shape((width, tokens), F32)
    dma = pltpu.SemaphoreType.DMA

    pieces = max(1, shard_len // 256)
    own = call(
        functools.partial(pick_kernel, pieces),
        shape((tokens, key_width), BF16),
        [HBM, HBM],
        [
            pltpu.VMEM((1, tokens), jnp.int32),
            pltpu.VMEM((shard_len, key_width), BF16),
            dma((pieces + 1,)),
        ],
    )(vis_pos, value_grad)
    own_all = [own] + [swap(own, "seq", peers, k) for k in range(1, peers)]

    stats, projt, residt, gaint, meant, weight = call(
        load_kernel,
        [row, tall, tall, tall, tall, shape(w_value.shape, BF16)],
        [HBM] * 6,
        [
            pltpu.SMEM((1, 2), jnp.int32),
            pltpu.VMEM((length, width), BF16),
            pltpu.VMEM((1, width), F32),
            pltpu.VMEM((tokens, width), BF16),
            pltpu.VMEM((tokens, width), BF16),
            dma((6,)),
        ],
    )(ques_span, ques_hidden, gain, vis_proj, vis_resid, w_value)

    scaledt, sums = call(
        functools.partial(norm_kernel, peers),
        [tall, row],
        [VMEM] * (peers + 4),
        [pltpu.VMEM((key_width, tokens), BF16)],
    )(*own_all, stats, weight, gaint, projt)
    sums_all = [sums] + [swap(sums, "seq", peers, k) for k in range(1, peers)]

    chunks = chunk_rows(w_down.shape[0] // peers)

    def weights_scratch(rows):
        copies = peers * (rows // min(rows, 256))
        return [pltpu.VMEM((peers * rows, width), BF16), dma((copies,))]

    def first_chunk():
        rows = chunks[0]
        gradt, logit, *partial = call(
            functools.partial(gate_kernel, features, peers, 0, rows),
            [shape((width, tokens), BF16), row] + [shape((rows, tokens), BF16)] * peers,
            [VMEM] * (peers + 4) + [HBM],
            weights_scratch(rows),
        )(*sums_all, projt, residt, scaledt, meant, w_down)
        return gradt, logit, partial

    def next_chunk(base, rows, after):
        return call(
            functools.partial(down_kernel, peers, base, rows, len(after)),
            [shape((rows, tokens), BF16)] * peers,
            [HBM, VMEM] + [ANY] * len(after),
            weights_scratch(rows),
        )(w_down, gradt, *after)

    def reduce(partial):
        return [partial[0]] + [swap(partial[k], "seq", peers, k) for k in range(1, peers)]

    paired = capacity % 16 == 0 and owners_count % 2 == 0
    halves = 2 if paired else 1

    def route(parts, after):
        rows = parts[0].shape[0]
        placed = call(
            functools.partial(place_kernel, capacity, owners_count, halves, len(parts)),
            [shape((slots // halves, rows), BF16)] * halves,
            [HBM] + [VMEM] * len(parts) + [ANY] * len(after),
            [pltpu.VMEM((1, tokens), jnp.int32), dma((1,))],
        )(owner, *parts, *after)
        if not paired:
            order = jnp.arange(owners_count) ^ lax.axis_index("frame")
            split = placed[0].reshape(owners_count, capacity, rows)[order]
            split = lax.all_to_all(split, "frame", split_axis=0, concat_axis=0, tiled=True)
            return [split[order].reshape(slots, rows)]
        same, other = placed
        other = swap(other, "frame", owners_count, 1)
        pairs = owners_count // 2
        grouped = call(
            functools.partial(group_kernel, capacity),
            [shape((2 * capacity, rows), BF16)] * pairs,
            [VMEM, VMEM],
        )(same, other)
        return [grouped[0]] + [
            swap(grouped[k], "frame", owners_count, 2 * k) for k in range(1, pairs)
        ]

    def finish(parts, base, rows, held):
        return call(
            functools.partial(final_kernel, capacity, base, len(parts)),
            shape(pre_owned.shape, BF16),
            [VMEM] * len(parts) + [HBM] + [HBM] * len(held),
            [
                pltpu.VMEM((rows, slots), BF16),
                pltpu.VMEM((rows, slots), BF16),
                dma((2,)),
            ],
            {len(parts) + 1: 0} if held else None,
            HBM,
        )(*parts, pre_owned, *held)

    bases = [sum(chunks[:i]) for i in range(len(chunks))]
    gradt, logit, partial = first_chunk()
    waiting = [reduce(partial), reduce(next_chunk(bases[1], chunks[1], []))]
    routed = []
    for index in range(len(chunks)):
        after = []
        if index == len(chunks) - 1:
            ques_grad = call(
                ques_kernel,
                shape(ques_hidden.shape, BF16),
                [HBM, VMEM, HBM, ANY],
                [
                    pltpu.SMEM((1, 2), jnp.int32),
                    pltpu.VMEM((tokens, width), BF16),
                    dma((2,)),
                ],
            )(ques_span, logit, vis_proj, routed[-1][0])
            after = [ques_grad]
        routed.append(route(waiting[index], after))
        if index + 2 < len(chunks):
            ahead = index + 2
            waiting.append(reduce(next_chunk(bases[ahead], chunks[ahead], [routed[-1][0]])))
    held = []
    for index in range(len(chunks)):
        held = [finish(routed[index], bases[index], chunks[index], held)]
    return (held[0], ques_grad)


def solution(mesh):
    in_specs = (
        P("frame", "seq", None),
        P("seq", None),
        P("seq"),
        P("frame", None),
        P("frame", None, None),
        P("frame", None),
        P("frame", None, "seq"),
        P("frame", None, "seq"),
        P("frame", None, "seq"),
        P(None, "seq"),
        P("frame", "seq", None),
    )
    out_specs = (P("frame", "seq", None), P("frame", None, "seq"))
    run = functools.partial(body, mesh.shape["seq"], mesh.shape["frame"])
    return jax.shard_map(run, mesh=mesh, in_specs=in_specs, out_specs=out_specs, check_vma=False)
```

time: 151 us -> 97.9 us (0.65)
  blocking collectives: 51.7 us -> 0 us
  starting transfers between devices: 0.04 us -> 38.9 us
  Pallas kernels: 0 us -> 28 us
  waiting for transfers between devices: 47.3 us -> 20.9 us
  matrix products: 23.2 us -> 0 us
  between operations: 16.2 us -> 1.06 us
  other arithmetic: 7.35 us -> 0 us
  local copies, waits for them, and re-layouts: 5.19 us -> 8.73 us
    reduce_scatter x1 -> x0, waiting for transfers between devices: 47.3 us -> none  [body(): lax.psum_scatter(jnp.einsum('hd,nd->hn', w_down, incoming, preferred_elem...]
    ppermute x0 -> x27, starting transfers between devices: none -> 38.9 us  [swap(): return lax.ppermute(value, axis, [(i, i ^ step) for i in range(count)])]
    all_to_all x1 -> x0, blocking collectives: 31.3 us -> none  [body(): lax.all_to_all(outgoing, 'frame', split_axis=0, concat_axis=0, tiled=True)]
    pallas_call x0 -> x16, Pallas kernels: none -> 28 us  [the longest x2 13.1 us: next_chunk(): call(functools.partial(down_kernel, peers, base, rows, len(after)), [shap...]
    dot_general x5 -> x0, matrix products: 23.2 us -> none  [the longest x1 16.6 us: body(): jnp.einsum('hd,nd->hn', w_down, incoming, preferred_element_type=jnp.floa...]
    ppermute x0 -> x27, waiting for transfers between devices: none -> 20.9 us  [swap(): return lax.ppermute(value, axis, [(i, i ^ step) for i in range(count)])]
    all_gather x1 -> x0, blocking collectives: 11.5 us -> none  [body(): lax.all_gather(own_piece, 'seq', axis=0, tiled=True).astype(jnp.float32)]
    psum x1 -> x0, blocking collectives: 8.94 us -> none  [body(): sum_query, sum_square = lax.psum((sum_query, sum_square), 'seq')]
  transfers between devices with their start and end apart: 1 -> 27, of which waited for: 1 -> 10; matrix products, arithmetic and copies ran while one was open for 2% -> 0% of each run, Pallas kernels for 0% -> 20%
where the time goes in v1:
time: 97.9 us; the launch traced here: 97.5 us
  starting transfers between devices  38.9 us (40%)
  Pallas kernels  28 us (29%)
  waiting for transfers between devices  20.9 us (21%)
  local copies, waits for them, and re-layouts  8.73 us (9%)
  between operations  1.06 us (1%)
    ppermute x27, starting transfers between devices, swap(): return lax.ppermute(value, axis, [(i, i ^ step) for i in range(count)])  38.9 us
    ppermute x27, waiting for transfers between devices, swap(): return lax.ppermute(value, axis, [(i, i ^ step) for i in range(count)])  20.9 us
    pallas_call x2, Pallas kernels, next_chunk(): call(functools.partial(down_kernel, peers, base, rows, len(after)), [shap...  13.1 us
    unnamed x26, local copies, waits for them, and re-layouts  8.73 us
    pallas_call x1, Pallas kernels, first_chunk(): call(functools.partial(gate_kernel, features, peers, 0, rows), [shape((wi...  4.71 us
    pallas_call x3, Pallas kernels, finish(): call(functools.partial(final_kernel, capacity, base, len(parts)), shape(p...  4.49 us
  transfers between devices with their start and end apart: 27, of which 10 were waited for; matrix products, arithmetic and copies ran while one was open for 0% of the time, Pallas kernels for 20%

profile of v1, /device:TPU:0, one launch (start us, length us, event | category | flops | bytes accessed | tf_op | source)
XLA Modules:
  0.0 97.5 jit_solution(5283783666262447280)
XLA Ops:
  3.2 4.0 %collective-permute-start.2 = (bf16[128,512]{1,0:T(8,128)(2,1)S(1)}, bf16[128,512]{1,0:T(8,128)(2,1)S(1)}, u32[]{:S(2)}, u32[]{:S(2)}) collective-permute-start(bf16[128,512]{1,0:T(8,128)(2,1)S(1)} %shard_map.122.refs_0_), channel_id=1, source_target_pairs={{0,24},{8,16},{16,8},{24,0},{1,25},{9,17},{17,9},{25,1},{2,26},{10... | collective-permute-start | bytes 393224 | tf_op jit(solution)/shard_map/ppermute | solution.py:39
  7.8 1.6 %copy-done.1 = bf16[2048,512]{1,0:T(8,128)(2,1)S(1)} copy-done((bf16[2048,512]{1,0:T(8,128)(2,1)S(1)}, bf16[2048,512]{1,0:T(8,128)(2,1)}, u32[]{:S(2)}) %copy-start.1) | copy-done | bytes 2097176
  13.7 1.5 %shard_map.123 = (f32[8,128]{1,0:T(8,128)S(1)}, f32[2048,128]{1,0:T(8,128)S(1)}, f32[2048,128]{1,0:T(8,128)S(1)}, f32[2048,128]{1,0:T(8,128)S(1)}, f32[2048,128]...) custom-call(s32[1,2]{1,0:T(1,128)S(1)} %copy-done.10, bf16[1,32,2048]{2,1,0:T(8,128)(2,1)S(1)} %copy-done.7, ...), custom_call_target="tpu_custom_call" | custom-call | flops 1024 | bytes 1024 | tf_op jit(solution)/shard_map/pallas_call | solution.py:351
  16.1 2.9 %collective-permute-start.5 = (f32[8,128]{1,0:T(8,128)S(1)}, f32[8,128]{1,0:T(8,128)S(1)}, u32[]{:S(2)}, u32[]{:S(2)}) collective-permute-start(f32[8,128]{1,0:T(8,128)S(1)} %get-tuple-element.46.refs_0_), channel_id=1, source_target_pairs={{0,24},{8,16},{16,8},{24,0},{1,25},{9,17},{17,9},{25,1},{2,26},{10... | collective-permute-start | bytes 12296 | tf_op jit(solution)/shard_map/ppermute | solution.py:39
  20.7 1.9 %collective-permute-done.4.refs_2_ = f32[8,128]{1,0:T(8,128)S(1)} collective-permute-done((f32[8,128]{1,0:T(8,128)S(1)}, f32[8,128]{1,0:T(8,128)S(1)}, u32[]{:S(2)}, u32[]{:S(2)}) %collective-permute-start.4) | collective-permute-done | bytes 4128 | tf_op jit(solution)/shard_map/ppermute | solution.py:39
  23.1 4.7 %shard_map.125 = (bf16[2048,128]{1,0:T(8,128)(2,1)S(1)}, f32[8,128]{1,0:T(8,128)S(1)}, bf16[512,128]{1,0:T(8,128)(2,1)S(1)}, bf16[512,128]{1,0:T(8,128)(2,1)S(1)...) custom-call(f32[8,128]{1,0:T(8,128)S(1)} %get-tuple-element.46.refs_0_, ...), custom_call_target="tpu_custom_call" | custom-call | flops 1024 | bytes 1024 | tf_op jit(solution)/shard_map/pallas_call | solution.py:381
  28.1 1.9 %collective-permute-start.7 = (bf16[512,128]{1,0:T(8,128)(2,1)S(1)}, bf16[512,128]{1,0:T(8,128)(2,1)S(1)}, u32[]{:S(2)}, u32[]{:S(2)}) collective-permute-start(bf16[512,128]{1,0:T(8,128)(2,1)S(1)} %get-tuple-element.53), channel_id=1, source_target_pairs={{0,16},{8,24},{16,0},{24,8},{1,17},{9,25},{17,1},{25,9},{2,18},{10... | collective-permute-start | bytes 393224 | tf_op jit(solution)/shard_map/ppermute | solution.py:39
  31.4 6.5 %shard_map.129 = (bf16[768,128]{1,0:T(8,128)(2,1)S(1)}, bf16[768,128]{1,0:T(8,128)(2,1)S(1)}, bf16[768,128]{1,0:T(8,128)(2,1)S(1)}, bf16[768,128]{1,0:T(8,128)(2,1)S(1)}) custom-call(bf16[8192,2048]{1,0:T(8,128)(2,1)} %refs_0_.3, bf16[2048,128]{1,0:T(8,128)(2,1)S(1)} %get-tuple-element.50.refs_1_), custom_call_target="tpu_custom_call" | custom-call | flops 1024 | bytes 1024 | tf_op jit(solution)/shard_map/pallas_call | solution.py:390
  38.1 1.9 %collective-permute-start.14 = (bf16[768,128]{1,0:T(8,128)(2,1)S(1)}, bf16[768,128]{1,0:T(8,128)(2,1)S(1)}, u32[]{:S(2)}, u32[]{:S(2)}) collective-permute-start(bf16[768,128]{1,0:T(8,128)(2,1)S(1)} %get-tuple-element.65), channel_id=1, source_target_pairs={{0,16},{8,24},{16,0},{24,8},{1,17},{9,25},{17,1},{25,9},{2,18},{10... | collective-permute-start | bytes 589832 | tf_op jit(solution)/shard_map/ppermute | solution.py:39
  41.9 1.7 %collective-permute-done.13.refs_2_ = bf16[768,128]{1,0:T(8,128)(2,1)S(1)} collective-permute-done((bf16[768,128]{1,0:T(8,128)(2,1)S(1)}, bf16[768,128]{1,0:T(8,128)(2,1)S(1)}, u32[]{:S(2)}, u32[]{:S(2)}) %collective-permute-start.13) | collective-permute-done | bytes 196640 | tf_op jit(solution)/shard_map/ppermute | solution.py:39
  43.6 1.7 %collective-permute-done.14.refs_3_ = bf16[768,128]{1,0:T(8,128)(2,1)S(1)} collective-permute-done((bf16[768,128]{1,0:T(8,128)(2,1)S(1)}, bf16[768,128]{1,0:T(8,128)(2,1)S(1)}, u32[]{:S(2)}, u32[]{:S(2)}) %collective-permute-start.14) | collective-permute-done | bytes 196640 | tf_op jit(solution)/shard_map/ppermute | solution.py:39
  47.2 6.7 %shard_map.128 = (bf16[768,128]{1,0:T(8,128)(2,1)S(1)}, bf16[768,128]{1,0:T(8,128)(2,1)S(1)}, bf16[768,128]{1,0:T(8,128)(2,1)S(1)}, bf16[768,128]{1,0:T(8,128)(2,1)S(1)}) custom-call(bf16[8192,2048]{1,0:T(8,128)(2,1)} %refs_0_.3, bf16[2048,128]{1,0:T(8,128)(2,1)S(1)} %get-tuple-element.50.refs_1_, bf16[64,512]{1,0:T(8,128)(2,1)S(1)} %get-tuple-element.57.refs_2_.refs_0_), custom_call_target="tpu_custom_call" | custom-call | flops 1024 | bytes 1024 | tf_op jit(solution)/shard_map/pallas_call | solution.py:390
  57.5 1.5 %shard_map.132.refs_5_ = bf16[1,32,2048]{2,1,0:T(8,128)(2,1)} custom-call(s32[1,2]{1,0:T(1,128)S(1)} %copy-done.11, f32[8,128]{1,0:T(8,128)S(1)} %get-tuple-element.62.logit_ref, bf16[1,128,2048]{2,1,0:T(8,128)(2,1)S(1)} %copy-done.3, bf16[64,768]{1,0:T(8,128)(2,1)S(1)} %get-tuple-element.69.after_ref.refs_0_), custom_call_target="tpu_custom_call" | custom-call | flops 1024 | bytes 1024 | tf_op jit(solution)/shard_map/pallas_call | solution.py:449
  59.0 2.7 %collective-permute-done.10.refs_2_ = bf16[768,128]{1,0:T(8,128)(2,1)S(1)} collective-permute-done((bf16[768,128]{1,0:T(8,128)(2,1)S(1)}, bf16[768,128]{1,0:T(8,128)(2,1)S(1)}, u32[]{:S(2)}, u32[]{:S(2)}) %collective-permute-start.10) | collective-permute-done | bytes 196640 | tf_op jit(solution)/shard_map/ppermute | solution.py:39
  61.7 4.9 %collective-permute-done.11.refs_3_ = bf16[768,128]{1,0:T(8,128)(2,1)S(1)} collective-permute-done((bf16[768,128]{1,0:T(8,128)(2,1)S(1)}, bf16[768,128]{1,0:T(8,128)(2,1)S(1)}, u32[]{:S(2)}, u32[]{:S(2)}) %collective-permute-start.11) | collective-permute-done | bytes 196640 | tf_op jit(solution)/shard_map/ppermute | solution.py:39
  68.0 1.6 %collective-permute-start.21 = (bf16[64,768]{1,0:T(8,128)(2,1)S(1)}, bf16[64,768]{1,0:T(8,128)(2,1)S(1)}, u32[]{:S(2)}, u32[]{:S(2)}) collective-permute-start(bf16[64,768]{1,0:T(8,128)(2,1)S(1)} %get-tuple-element.76), channel_id=1, source_target_pairs={{0,2},{1,3},{2,0},{3,1},{4,6},{5,7},{6,4},{7,5},{8,10},{9,11},{10,... | collective-permute-start | bytes 294920 | tf_op jit(solution)/shard_map/ppermute | solution.py:39
  70.0 2.6 %collective-permute-start.25 = (bf16[64,512]{1,0:T(8,128)(2,1)S(1)}, bf16[64,512]{1,0:T(8,128)(2,1)S(1)}, u32[]{:S(2)}, u32[]{:S(2)}) collective-permute-start(bf16[64,512]{1,0:T(8,128)(2,1)S(1)} %get-tuple-element.80), channel_id=1, source_target_pairs={{0,4},{1,5},{2,6},{3,7},{4,0},{5,1},{6,2},{7,3},{8,12},{9,13},{10,... | collective-permute-start | bytes 196616 | tf_op jit(solution)/shard_map/ppermute | solution.py:39
  74.0 1.7 %collective-permute-start.22 = (bf16[64,768]{1,0:T(8,128)(2,1)S(1)}, bf16[64,768]{1,0:T(8,128)(2,1)S(1)}, u32[]{:S(2)}, u32[]{:S(2)}) collective-permute-start(bf16[64,768]{1,0:T(8,128)(2,1)S(1)} %get-tuple-element.77), channel_id=1, source_target_pairs={{0,4},{1,5},{2,6},{3,7},{4,0},{5,1},{6,2},{7,3},{8,12},{9,13},{10,... | collective-permute-start | bytes 294920 | tf_op jit(solution)/shard_map/ppermute | solution.py:39
  76.0 3.0 %collective-permute-start.23 = (bf16[64,768]{1,0:T(8,128)(2,1)S(1)}, bf16[64,768]{1,0:T(8,128)(2,1)S(1)}, u32[]{:S(2)}, u32[]{:S(2)}) collective-permute-start(bf16[64,768]{1,0:T(8,128)(2,1)S(1)} %get-tuple-element.78), channel_id=1, source_target_pairs={{0,6},{1,7},{2,4},{3,5},{4,2},{5,3},{6,0},{7,1},{8,14},{9,15},{10,... | collective-permute-start | bytes 294920 | tf_op jit(solution)/shard_map/ppermute | solution.py:39
  79.0 3.9 %collective-permute-start.18 = (bf16[64,768]{1,0:T(8,128)(2,1)S(1)}, bf16[64,768]{1,0:T(8,128)(2,1)S(1)}, u32[]{:S(2)}, u32[]{:S(2)}) collective-permute-start(bf16[64,768]{1,0:T(8,128)(2,1)S(1)} %get-tuple-element.73), channel_id=1, source_target_pairs={{0,2},{1,3},{2,0},{3,1},{4,6},{5,7},{6,4},{7,5},{8,10},{9,11},{10,... | collective-permute-start | bytes 294920 | tf_op jit(solution)/shard_map/ppermute | solution.py:39
  82.8 4.0 %collective-permute-start.19 = (bf16[64,768]{1,0:T(8,128)(2,1)S(1)}, bf16[64,768]{1,0:T(8,128)(2,1)S(1)}, u32[]{:S(2)}, u32[]{:S(2)}) collective-permute-start(bf16[64,768]{1,0:T(8,128)(2,1)S(1)} %get-tuple-element.74), channel_id=1, source_target_pairs={{0,4},{1,5},{2,6},{3,7},{4,0},{5,1},{6,2},{7,3},{8,12},{9,13},{10,... | collective-permute-start | bytes 294920 | tf_op jit(solution)/shard_map/ppermute | solution.py:39
  89.4 1.6 %shard_map.136.refs_5_ = bf16[1,2048,256]{2,1,0:T(8,128)(2,1)} custom-call(bf16[64,768]{1,0:T(8,128)(2,1)S(1)} %get-tuple-element.69.after_ref.refs_0_, bf16[64,768]{1,0:T(8,128)(2,1)S(1)} %collective-permute-done.21.refs_1_, bf16[64,768]{1,0:T(8,128)(2,1)S(1)} %collective-permute-done.22.refs_2_, ...), custom_call_target="tpu_custom_call", output_to_operand_aliasing={{}: (5, {})} | custom-call | flops 1024 | bytes 1024 | tf_op jit(solution)/shard_map/pallas_call | solution.py:429
  91.1 4.7 %collective-permute-done.19.refs_2_ = bf16[64,768]{1,0:T(8,128)(2,1)S(1)} collective-permute-done((bf16[64,768]{1,0:T(8,128)(2,1)S(1)}, bf16[64,768]{1,0:T(8,128)(2,1)S(1)}, u32[]{:S(2)}, u32[]{:S(2)}) %collective-permute-start.19) | collective-permute-done | bytes 98336 | tf_op jit(solution)/shard_map/ppermute | solution.py:39
  95.7 1.6 %shard_map.137 = bf16[1,2048,256]{2,1,0:T(8,128)(2,1)} custom-call(bf16[64,768]{1,0:T(8,128)(2,1)S(1)} %get-tuple-element.72.refs_0_, bf16[64,768]{1,0:T(8,128)(2,1)S(1)} %collective-permute-done.18.refs_1_, bf16[64,768]{1,0:T(8,128)(2,1)S(1)} %collective-permute-done.19.refs_2_, ...), custom_call_target="tpu_custom_call", output_to_operand_aliasing={{}: (5, {})} | custom-call | flops 1024 | bytes 1024 | tf_op jit(solution)/shard_map/pallas_call | solution.py:429
  (72 shorter events, 25.7 us)
Async XLA Ops:
  3.2 12.1 %collective-permute-start.2 = (bf16[128,512]{1,0:T(8,128)(2,1)S(1)}, bf16[128,512]{1,0:T(8,128)(2,1)S(1)}, u32[]{:S(2)}, u32[]{:S(2)}) collective-permute-start(bf16[128,512]{1,0:T(8,128)(2,1)S(1)} %shard_map.122.refs_0_), channel_id=1, source_target_pairs={{0,24},{8,16},{16,8},{24,0},{1,25},{9,17},{17,9},{25,1},{2,26},{10... | collective-permute-start | bytes 393224 | tf_op jit(solution)/shard_map/ppermute | solution.py:39
  7.1 8.1 %collective-permute-start.1 = (bf16[128,512]{1,0:T(8,128)(2,1)S(1)}, bf16[128,512]{1,0:T(8,128)(2,1)S(1)}, u32[]{:S(2)}, u32[]{:S(2)}) collective-permute-start(bf16[128,512]{1,0:T(8,128)(2,1)S(1)} %shard_map.122.refs_0_), channel_id=1, source_target_pairs={{0,16},{8,24},{16,0},{24,8},{1,17},{9,25},{17,1},{25,9},{2,18},{10... | collective-permute-start | bytes 393224 | tf_op jit(solution)/shard_map/ppermute | solution.py:39
  7.6 7.6 %collective-permute-start = (bf16[128,512]{1,0:T(8,128)(2,1)S(1)}, bf16[128,512]{1,0:T(8,128)(2,1)S(1)}, u32[]{:S(2)}, u32[]{:S(2)}) collective-permute-start(bf16[128,512]{1,0:T(8,128)(2,1)S(1)} %shard_map.122.refs_0_), channel_id=1, source_target_pairs={{0,8},{8,0},{16,24},{24,16},{1,9},{9,1},{17,25},{25,17},{2,10},{10... | collective-permute-start | bytes 393224 | tf_op jit(solution)/shard_map/ppermute | solution.py:39
  27.9 12.1 %collective-permute-start.6 = (bf16[512,128]{1,0:T(8,128)(2,1)S(1)}, bf16[512,128]{1,0:T(8,128)(2,1)S(1)}, u32[]{:S(2)}, u32[]{:S(2)}) collective-permute-start(bf16[512,128]{1,0:T(8,128)(2,1)S(1)} %get-tuple-element.52), channel_id=1, source_target_pairs={{0,8},{8,0},{16,24},{24,16},{1,9},{9,1},{17,25},{25,17},{2,10},{10... | collective-permute-start | bytes 393224 | tf_op jit(solution)/shard_map/ppermute | solution.py:39
  28.1 13.4 %collective-permute-start.7 = (bf16[512,128]{1,0:T(8,128)(2,1)S(1)}, bf16[512,128]{1,0:T(8,128)(2,1)S(1)}, u32[]{:S(2)}, u32[]{:S(2)}) collective-permute-start(bf16[512,128]{1,0:T(8,128)(2,1)S(1)} %get-tuple-element.53), channel_id=1, source_target_pairs={{0,16},{8,24},{16,0},{24,8},{1,17},{9,25},{17,1},{25,9},{2,18},{10... | collective-permute-start | bytes 393224 | tf_op jit(solution)/shard_map/ppermute | solution.py:39
  30.0 11.5 %collective-permute-start.8 = (bf16[512,128]{1,0:T(8,128)(2,1)S(1)}, bf16[512,128]{1,0:T(8,128)(2,1)S(1)}, u32[]{:S(2)}, u32[]{:S(2)}) collective-permute-start(bf16[512,128]{1,0:T(8,128)(2,1)S(1)} %get-tuple-element.54), channel_id=1, source_target_pairs={{0,24},{8,16},{16,8},{24,0},{1,25},{9,17},{17,9},{25,1},{2,26},{10... | collective-permute-start | bytes 393224 | tf_op jit(solution)/shard_map/ppermute | solution.py:39
  37.9 5.7 %collective-permute-start.13 = (bf16[768,128]{1,0:T(8,128)(2,1)S(1)}, bf16[768,128]{1,0:T(8,128)(2,1)S(1)}, u32[]{:S(2)}, u32[]{:S(2)}) collective-permute-start(bf16[768,128]{1,0:T(8,128)(2,1)S(1)} %get-tuple-element.64), channel_id=1, source_target_pairs={{0,8},{8,0},{16,24},{24,16},{1,9},{9,1},{17,25},{25,17},{2,10},{10... | collective-permute-start | bytes 589832 | tf_op jit(solution)/shard_map/ppermute | solution.py:39
  38.1 7.2 %collective-permute-start.14 = (bf16[768,128]{1,0:T(8,128)(2,1)S(1)}, bf16[768,128]{1,0:T(8,128)(2,1)S(1)}, u32[]{:S(2)}, u32[]{:S(2)}) collective-permute-start(bf16[768,128]{1,0:T(8,128)(2,1)S(1)} %get-tuple-element.65), channel_id=1, source_target_pairs={{0,16},{8,24},{16,0},{24,8},{1,17},{9,25},{17,1},{25,9},{2,18},{10... | collective-permute-start | bytes 589832 | tf_op jit(solution)/shard_map/ppermute | solution.py:39
  40.0 6.7 %collective-permute-start.15 = (bf16[768,128]{1,0:T(8,128)(2,1)S(1)}, bf16[768,128]{1,0:T(8,128)(2,1)S(1)}, u32[]{:S(2)}, u32[]{:S(2)}) collective-permute-start(bf16[768,128]{1,0:T(8,128)(2,1)S(1)} %get-tuple-element.66), channel_id=1, source_target_pairs={{0,24},{8,16},{16,8},{24,0},{1,25},{9,17},{17,9},{25,1},{2,26},{10... | collective-permute-start | bytes 589832 | tf_op jit(solution)/shard_map/ppermute | solution.py:39
  41.8 5.4 %collective-permute-start.9 = (bf16[128,512]{1,0:T(8,128)(2,1)S(1)}, bf16[128,512]{1,0:T(8,128)(2,1)S(1)}, u32[]{:S(2)}, u32[]{:S(2)}) collective-permute-start(bf16[128,512]{1,0:T(8,128)(2,1)S(1)} %get-tuple-element.56), channel_id=1, source_target_pairs={{0,1},{1,0},{2,3},{3,2},{4,5},{5,4},{6,7},{7,6},{8,9},{9,8},{10,11... | collective-permute-start | bytes 393224 | tf_op jit(solution)/shard_map/ppermute | solution.py:39
  47.1 10.4 %collective-permute-start.16 = (bf16[128,768]{1,0:T(8,128)(2,1)S(1)}, bf16[128,768]{1,0:T(8,128)(2,1)S(1)}, u32[]{:S(2)}, u32[]{:S(2)}) collective-permute-start(bf16[128,768]{1,0:T(8,128)(2,1)S(1)} %get-tuple-element.68), channel_id=1, source_target_pairs={{0,1},{1,0},{2,3},{3,2},{4,5},{5,4},{6,7},{7,6},{8,9},{9,8},{10,11... | collective-permute-start | bytes 589832 | tf_op jit(solution)/shard_map/ppermute | solution.py:39
  53.9 7.8 %collective-permute-start.10 = (bf16[768,128]{1,0:T(8,128)(2,1)S(1)}, bf16[768,128]{1,0:T(8,128)(2,1)S(1)}, u32[]{:S(2)}, u32[]{:S(2)}) collective-permute-start(bf16[768,128]{1,0:T(8,128)(2,1)S(1)} %get-tuple-element.59), channel_id=1, source_target_pairs={{0,8},{8,0},{16,24},{24,16},{1,9},{9,1},{17,25},{25,17},{2,10},{10... | collective-permute-start | bytes 589832 | tf_op jit(solution)/shard_map/ppermute | solution.py:39
  55.4 11.2 %collective-permute-start.11 = (bf16[768,128]{1,0:T(8,128)(2,1)S(1)}, bf16[768,128]{1,0:T(8,128)(2,1)S(1)}, u32[]{:S(2)}, u32[]{:S(2)}) collective-permute-start(bf16[768,128]{1,0:T(8,128)(2,1)S(1)} %get-tuple-element.60), channel_id=1, source_target_pairs={{0,16},{8,24},{16,0},{24,8},{1,17},{9,25},{17,1},{25,9},{2,18},{10... | collective-permute-start | bytes 589832 | tf_op jit(solution)/shard_map/ppermute | solution.py:39
  56.6 10.0 %collective-permute-start.12 = (bf16[768,128]{1,0:T(8,128)(2,1)S(1)}, bf16[768,128]{1,0:T(8,128)(2,1)S(1)}, u32[]{:S(2)}, u32[]{:S(2)}) collective-permute-start(bf16[768,128]{1,0:T(8,128)(2,1)S(1)} %get-tuple-element.61), channel_id=1, source_target_pairs={{0,24},{8,16},{16,8},{24,0},{1,25},{9,17},{17,9},{25,1},{2,26},{10... | collective-permute-start | bytes 589832 | tf_op jit(solution)/shard_map/ppermute | solution.py:39
  67.9 6.1 %collective-permute-start.17 = (bf16[128,768]{1,0:T(8,128)(2,1)S(1)}, bf16[128,768]{1,0:T(8,128)(2,1)S(1)}, u32[]{:S(2)}, u32[]{:S(2)}) collective-permute-start(bf16[128,768]{1,0:T(8,128)(2,1)S(1)} %get-tuple-element.71), channel_id=1, source_target_pairs={{0,1},{1,0},{2,3},{3,2},{4,5},{5,4},{6,7},{7,6},{8,9},{9,8},{10,11... | collective-permute-start | bytes 589832 | tf_op jit(solution)/shard_map/ppermute | solution.py:39
  68.0 18.8 %collective-permute-start.21 = (bf16[64,768]{1,0:T(8,128)(2,1)S(1)}, bf16[64,768]{1,0:T(8,128)(2,1)S(1)}, u32[]{:S(2)}, u32[]{:S(2)}) collective-permute-start(bf16[64,768]{1,0:T(8,128)(2,1)S(1)} %get-tuple-element.76), channel_id=1, source_target_pairs={{0,2},{1,3},{2,0},{3,1},{4,6},{5,7},{6,4},{7,5},{8,10},{9,11},{10,... | collective-permute-start | bytes 294920 | tf_op jit(solution)/shard_map/ppermute | solution.py:39
  69.6 6.4 %collective-permute-start.24 = (bf16[64,512]{1,0:T(8,128)(2,1)S(1)}, bf16[64,512]{1,0:T(8,128)(2,1)S(1)}, u32[]{:S(2)}, u32[]{:S(2)}) collective-permute-start(bf16[64,512]{1,0:T(8,128)(2,1)S(1)} %get-tuple-element.79), channel_id=1, source_target_pairs={{0,2},{1,3},{2,0},{3,1},{4,6},{5,7},{6,4},{7,5},{8,10},{9,11},{10,... | collective-permute-start | bytes 196616 | tf_op jit(solution)/shard_map/ppermute | solution.py:39
  70.0 8.9 %collective-permute-start.25 = (bf16[64,512]{1,0:T(8,128)(2,1)S(1)}, bf16[64,512]{1,0:T(8,128)(2,1)S(1)}, u32[]{:S(2)}, u32[]{:S(2)}) collective-permute-start(bf16[64,512]{1,0:T(8,128)(2,1)S(1)} %get-tuple-element.80), channel_id=1, source_target_pairs={{0,4},{1,5},{2,6},{3,7},{4,0},{5,1},{6,2},{7,3},{8,12},{9,13},{10,... | collective-permute-start | bytes 196616 | tf_op jit(solution)/shard_map/ppermute | solution.py:39
  72.6 10.2 %collective-permute-start.26 = (bf16[64,512]{1,0:T(8,128)(2,1)S(1)}, bf16[64,512]{1,0:T(8,128)(2,1)S(1)}, u32[]{:S(2)}, u32[]{:S(2)}) collective-permute-start(bf16[64,512]{1,0:T(8,128)(2,1)S(1)} %get-tuple-element.81), channel_id=1, source_target_pairs={{0,6},{1,7},{2,4},{3,5},{4,2},{5,3},{6,0},{7,1},{8,14},{9,15},{10,... | collective-permute-start | bytes 196616 | tf_op jit(solution)/shard_map/ppermute | solution.py:39
  74.0 15.4 %collective-permute-start.22 = (bf16[64,768]{1,0:T(8,128)(2,1)S(1)}, bf16[64,768]{1,0:T(8,128)(2,1)S(1)}, u32[]{:S(2)}, u32[]{:S(2)}) collective-permute-start(bf16[64,768]{1,0:T(8,128)(2,1)S(1)} %get-tuple-element.77), channel_id=1, source_target_pairs={{0,4},{1,5},{2,6},{3,7},{4,0},{5,1},{6,2},{7,3},{8,12},{9,13},{10,... | collective-permute-start | bytes 294920 | tf_op jit(solution)/shard_map/ppermute | solution.py:39
  76.0 13.4 %collective-permute-start.23 = (bf16[64,768]{1,0:T(8,128)(2,1)S(1)}, bf16[64,768]{1,0:T(8,128)(2,1)S(1)}, u32[]{:S(2)}, u32[]{:S(2)}) collective-permute-start(bf16[64,768]{1,0:T(8,128)(2,1)S(1)} %get-tuple-element.78), channel_id=1, source_target_pairs={{0,6},{1,7},{2,4},{3,5},{4,2},{5,3},{6,0},{7,1},{8,14},{9,15},{10,... | collective-permute-start | bytes 294920 | tf_op jit(solution)/shard_map/ppermute | solution.py:39
  79.0 12.1 %collective-permute-start.18 = (bf16[64,768]{1,0:T(8,128)(2,1)S(1)}, bf16[64,768]{1,0:T(8,128)(2,1)S(1)}, u32[]{:S(2)}, u32[]{:S(2)}) collective-permute-start(bf16[64,768]{1,0:T(8,128)(2,1)S(1)} %get-tuple-element.73), channel_id=1, source_target_pairs={{0,2},{1,3},{2,0},{3,1},{4,6},{5,7},{6,4},{7,5},{8,10},{9,11},{10,... | collective-permute-start | bytes 294920 | tf_op jit(solution)/shard_map/ppermute | solution.py:39
  82.8 12.9 %collective-permute-start.19 = (bf16[64,768]{1,0:T(8,128)(2,1)S(1)}, bf16[64,768]{1,0:T(8,128)(2,1)S(1)}, u32[]{:S(2)}, u32[]{:S(2)}) collective-permute-start(bf16[64,768]{1,0:T(8,128)(2,1)S(1)} %get-tuple-element.74), channel_id=1, source_target_pairs={{0,4},{1,5},{2,6},{3,7},{4,0},{5,1},{6,2},{7,3},{8,12},{9,13},{10,... | collective-permute-start | bytes 294920 | tf_op jit(solution)/shard_map/ppermute | solution.py:39
  86.8 8.9 %collective-permute-start.20 = (bf16[64,768]{1,0:T(8,128)(2,1)S(1)}, bf16[64,768]{1,0:T(8,128)(2,1)S(1)}, u32[]{:S(2)}, u32[]{:S(2)}) collective-permute-start(bf16[64,768]{1,0:T(8,128)(2,1)S(1)} %get-tuple-element.75), channel_id=1, source_target_pairs={{0,6},{1,7},{2,4},{3,5},{4,2},{5,3},{6,0},{7,1},{8,14},{9,15},{10,... | collective-permute-start | bytes 294920 | tf_op jit(solution)/shard_map/ppermute | solution.py:39
  (16 other events, 85.4 us)
